TPU v7x, 512 devices: a whole 4x4x16 slice. The times are simulated.
512 devices in a mesh: factor: 32 (over x, z_hi, core), rows: 16 (over z_lo, y).
Axes of the slice: x: 4, y: 4, z: 16 (z_hi: 4, z_lo: 4; z = z_hi * 4 + z_lo), core: 2. Of those that a mesh axis runs over, the one named last changes fastest.
Arguments:
- working: bfloat16 [16384, 16384], P('rows', 'factor'), may hold values from -30 to 30, as said below
- levels: int32 [3, 32, 512], P(None, 'factor'), may hold values from 0 to 511, each once within a row
Outputs:
- rotated: bfloat16 [16384, 16384], P('rows', 'factor')
Inputs may be any that keep to these rules, and one draw needn't show every extreme that they name: `working`: entries of order one; column scales differ over the columns. Each row levels[s, p, :] is a permutation of 0 to 511.
All inputs are finite; a program needn't handle non-finite values.
Results may differ from a plain program's by a relative error of at most 0.013.
The roundings to bfloat16 on the way count: a program that leaves them out, or rounds other values in their place, can miss the bound.
Values may be sent and summed in bfloat16 or wider, within the bound.
A program may use at most 64 MiB of HBM per device.

v0:
```python
import math

import jax
import jax.numpy as jnp
from jax import lax
from jax.sharding import PartitionSpec as P


def passed_along(value, axis, by):
    count = lax.axis_size(axis)
    pairs = [(i, i + by) for i in range(count) if 0 <= i + by < count]
    return lax.ppermute(value, axis, pairs)


def inner_rows(left, right):
    return lax.dot_general(
        left, right, (((0,), (0,)), ((), ())), preferred_element_type=jnp.float32
    )


def body(working, levels):
    width = working.shape[1]
    half = width // 2
    sweeps = levels.shape[0]
    devices = lax.axis_size("factor")
    position = lax.axis_index("factor")
    for sweep in range(sweeps):
        gram = lax.psum(inner_rows(working, working), "rows")
        spectrum = 1.0 + levels[sweep, 0].astype(jnp.float32) / float(width)
        scaled = gram * spectrum[None, :]
        frobenius = jnp.sqrt(jnp.sum(scaled * scaled) + 1e-06)
        start = scaled * (0.5 * math.sqrt(width) / frobenius)
        inner = jnp.dot(start.T, start, precision=lax.Precision.HIGHEST)
        correct = 1.5 * jnp.eye(width, dtype=jnp.float32) - 0.5 * inner
        rotation = jnp.dot(start, correct, precision=lax.Precision.HIGHEST).astype(jnp.bfloat16)
        moved = jnp.dot(working, rotation, preferred_element_type=jnp.float32)
        working = moved.astype(jnp.bfloat16)
        if sweep + 1 < sweeps:
            upper = working[:, :half]
            lower = working[:, half:]
            outgoing = jnp.where(position == 0, lower, upper)
            from_before = passed_along(outgoing, "factor", 1)
            from_after = passed_along(lower, "factor", -1)
            new_upper = jnp.where(position == 0, upper, from_before)
            new_lower = jnp.where(position == devices - 1, upper, from_after)
            working = jnp.concatenate([new_upper, new_lower], axis=1)
    return working


def solution(mesh):
    placed = (P("rows", "factor"), P(None, "factor", None))
    return jax.shard_map(
        body, mesh=mesh, in_specs=placed, out_specs=P("rows", "factor"), check_vma=False
    )
```

profile of v0, /device:TPU:1, one launch (start us, length us, event | category | flops | bytes accessed | tf_op | source)
XLA Modules:
  0.0 612.5 jit_solution(1164938040517289869)
XLA Ops:
  7.8 1.7 fusion.31
  10.2 168.6 %all-reduce.4.cloned.1.call-done = f32[512,512]{1,0:T(8,128)} async-done(((f32[512,512]{1,0:T(8,128)}), f32[512,512]{1,0:T(8,128)}) %all-reduce.4.cloned.1.call-update) | async-done | bytes 1048592 | tf_op jit(solution)/shard_map/psum | solution.py:28
  178.7 2.2 multiply_reduce_fusion.2
  181.6 1.9 select_subtract_fusion.2
  183.6 1.9 convolution_convert_fusion.5
  187.1 18.3 %collective-permute-start = (bf16[1024,256]{0,1:T(8,128)(2,1)}, bf16[1024,256]{0,1:T(8,128)(2,1)S(1)}, u32[]{:S(2)}, u32[]{:S(2)}) collective-permute-start(bf16[1024,256]{0,1:T(8,128)(2,1)} %get-tuple-element.11), channel_id=1, source_target_pairs={{0,16},{16,32},{32,48},{48,64},{64,80},{80,96},{96,112},{112,128},... | collective-permute-start | bytes 1572872 | tf_op jit(solution)/shard_map/ppermute | solution.py:12
  205.4 1.9 collective-permute-start.1
  207.3 13.3 %collective-permute-done = bf16[1024,256]{0,1:T(8,128)(2,1)S(1)} collective-permute-done((bf16[1024,256]{0,1:T(8,128)(2,1)}, bf16[1024,256]{0,1:T(8,128)(2,1)S(1)}, u32[]{:S(2)}, u32[]{:S(2)}) %collective-permute-start) | collective-permute-done | bytes 524320 | tf_op jit(solution)/shard_map/ppermute | solution.py:12
  221.5 9.5 %collective-permute-done.1 = bf16[1024,256]{0,1:T(8,128)(2,1)} collective-permute-done((bf16[1024,256]{0,1:T(8,128)(2,1)S(1)}, bf16[1024,256]{0,1:T(8,128)(2,1)}, u32[]{:S(2)}, u32[]{:S(2)}) %collective-permute-start.1) | collective-permute-done | bytes 524320 | tf_op jit(solution)/shard_map/ppermute | solution.py:12
  232.2 1.7 fusion.14
  234.0 155.1 %all-reduce.6.cloned.1.call-done = f32[512,512]{1,0:T(8,128)} async-done(((f32[512,512]{1,0:T(8,128)}), f32[512,512]{1,0:T(8,128)}) %all-reduce.6.cloned.1.call-update) | async-done | bytes 1048592 | tf_op jit(solution)/shard_map/psum | solution.py:28
  389.1 2.2 multiply_reduce_fusion.1
  392.0 1.9 select_subtract_fusion.1
  394.0 1.9 convolution_convert_fusion.4
  396.7 18.3 %collective-permute-start.2 = (bf16[1024,256]{0,1:T(8,128)(2,1)S(1)}, bf16[1024,256]{0,1:T(8,128)(2,1)S(1)}, u32[]{:S(2)}, u32[]{:S(2)}) collective-permute-start(bf16[1024,256]{0,1:T(8,128)(2,1)S(1)} %get-tuple-element.7), channel_id=1, source_target_pairs={{0,16},{16,32},{32,48},{48,64},{64,80},{80,96},{96,112},{112,128},... | collective-permute-start | bytes 1572872 | tf_op jit(solution)/shard_map/ppermute | solution.py:12
  415.0 2.1 collective-permute-start.3
  417.1 12.8 %collective-permute-done.2 = bf16[1024,256]{0,1:T(8,128)(2,1)S(1)} collective-permute-done((bf16[1024,256]{0,1:T(8,128)(2,1)S(1)}, bf16[1024,256]{0,1:T(8,128)(2,1)S(1)}, u32[]{:S(2)}, u32[]{:S(2)}) %collective-permute-start.2) | collective-permute-done | bytes 524320 | tf_op jit(solution)/shard_map/ppermute | solution.py:12
  430.0 10.5 %collective-permute-done.3 = bf16[1024,256]{0,1:T(8,128)(2,1)S(1)} collective-permute-done((bf16[1024,256]{0,1:T(8,128)(2,1)S(1)}, bf16[1024,256]{0,1:T(8,128)(2,1)S(1)}, u32[]{:S(2)}, u32[]{:S(2)}) %collective-permute-start.3) | collective-permute-done | bytes 524320 | tf_op jit(solution)/shard_map/ppermute | solution.py:12
  440.6 1.7 fusion.13
  442.4 155.1 %all-reduce.8.cloned.1.call-done = f32[512,512]{1,0:T(8,128)} async-done(((f32[512,512]{1,0:T(8,128)}), f32[512,512]{1,0:T(8,128)}) %all-reduce.8.cloned.1.call-update) | async-done | bytes 1048592 | tf_op jit(solution)/shard_map/psum | solution.py:28
  597.5 2.2 multiply_reduce_fusion
  600.4 1.9 select_subtract_fusion
  602.3 1.9 convolution_convert_fusion.3
  604.2 1.7 convolution_convert_fusion
  (25 shorter events, 6.7 us)
Async XLA Ops:
  6.5 1.2 copy-start
  6.5 172.2 %all-reduce.4.cloned.1.call-start = ((), (), s32[]{:S(2)}) async-start(), calls=%async_computation | async-start | bytes 2097152 | tf_op jit(solution)/shard_map/psum | solution.py:28
  9.5 0.7 copy-start.5
  9.5 379.6 %all-reduce.6.cloned.1.call-start = ((), (), s32[]{:S(2)}) async-start(), calls=%async_computation.1 | async-start | bytes 2097152 | tf_op jit(solution)/shard_map/psum | solution.py:28
  178.7 2.9 copy-start.1
  187.1 33.6 %collective-permute-start = (bf16[1024,256]{0,1:T(8,128)(2,1)}, bf16[1024,256]{0,1:T(8,128)(2,1)S(1)}, u32[]{:S(2)}, u32[]{:S(2)}) collective-permute-start(bf16[1024,256]{0,1:T(8,128)(2,1)} %get-tuple-element.11), channel_id=1, source_target_pairs={{0,16},{16,32},{32,48},{48,64},{64,80},{80,96},{96,112},{112,128},... | collective-permute-start | bytes 1572872 | tf_op jit(solution)/shard_map/ppermute | solution.py:12
  205.4 25.5 %collective-permute-start.1 = (bf16[1024,256]{0,1:T(8,128)(2,1)S(1)}, bf16[1024,256]{0,1:T(8,128)(2,1)}, u32[]{:S(2)}, u32[]{:S(2)}) collective-permute-start(bf16[1024,256]{0,1:T(8,128)(2,1)S(1)} %get-tuple-element.12), channel_id=1, source_target_pairs={{16,0},{32,16},{48,32},{64,48},{80,64},{96,80},{112,96},{128,112},... | collective-permute-start | bytes 1572872 | tf_op jit(solution)/shard_map/ppermute | solution.py:12
  220.7 0.8 copy-start.4
  234.0 363.5 %all-reduce.8.cloned.1.call-start = ((), (), s32[]{:S(2)}) async-start(), calls=%async_computation.2 | async-start | bytes 2097152 | tf_op jit(solution)/shard_map/psum | solution.py:28
  389.1 2.9 copy-start.3
  396.7 33.3 %collective-permute-start.2 = (bf16[1024,256]{0,1:T(8,128)(2,1)S(1)}, bf16[1024,256]{0,1:T(8,128)(2,1)S(1)}, u32[]{:S(2)}, u32[]{:S(2)}) collective-permute-start(bf16[1024,256]{0,1:T(8,128)(2,1)S(1)} %get-tuple-element.7), channel_id=1, source_target_pairs={{0,16},{16,32},{32,48},{48,64},{64,80},{80,96},{96,112},{112,128},... | collective-permute-start | bytes 1572872 | tf_op jit(solution)/shard_map/ppermute | solution.py:12
  415.0 25.4 %collective-permute-start.3 = (bf16[1024,256]{0,1:T(8,128)(2,1)S(1)}, bf16[1024,256]{0,1:T(8,128)(2,1)S(1)}, u32[]{:S(2)}, u32[]{:S(2)}) collective-permute-start(bf16[1024,256]{0,1:T(8,128)(2,1)S(1)} %get-tuple-element.8), channel_id=1, source_target_pairs={{16,0},{32,16},{48,32},{64,48},{80,64},{96,80},{112,96},{128,112},... | collective-permute-start | bytes 1572872 | tf_op jit(solution)/shard_map/ppermute | solution.py:12
  597.5 2.9 copy-start.2
Sparse Core Ops, SparseCore 0:
  10.3 168.4 all-reduce.3
  234.1 154.9 all-reduce.5
  442.5 154.9 all-reduce.7
where the time goes:
time: 622 us; the launch traced here: 613 us
  waiting for transfers between devices  525 us (84%)
  starting transfers between devices  40.7 us (7%)
  matrix products  19.9 us (3%)
  between operations  15.3 us (2%)
  other arithmetic  8.94 us (1%)
    psum x3, waiting for transfers between devices, body(): gram = lax.psum(inner_rows(working, working), 'rows')  479 us
    ppermute x4, waiting for transfers between devices, passed_along(): return lax.ppermute(value, axis, pairs)  46.1 us
    ppermute x4, starting transfers between devices, passed_along(): return lax.ppermute(value, axis, pairs)  40.6 us
  transfers between devices with their start and end apart: 7, of which 7 were waited for; matrix products, arithmetic and copies ran while one was open for 0% of the time, Pallas kernels for 0%

commit v1 on v0

v1 whole, which is shorter than its diff:
```python
import functools
import math

import jax
import jax.numpy as jnp
from jax import lax
from jax.experimental import pallas as pl
from jax.experimental.pallas import tpu as pltpu
from jax.sharding import PartitionSpec as P

MESH = pl.DeviceIdType.MESH
F32, BF16 = jnp.float32, jnp.bfloat16
Y_SIZE = 4
CHUNKS = 4


def inner_rows(left, right):
    return lax.dot_general(
        left, right, (((0,), (0,)), ((), ())), preferred_element_type=F32
    )


def mm(left, right):
    return jnp.dot(left, right, preferred_element_type=F32)


def halves(wide):
    high = wide.astype(BF16)
    return high, (wide - high.astype(F32)).astype(BF16)


def remote(src, dst, send, recv, **to):
    return pltpu.make_async_remote_copy(
        src_ref=src, dst_ref=dst, send_sem=send, recv_sem=recv, device_id=to, device_id_type=MESH
    )


def kernel(n_factor, n_rows, steps, working, levels, out,
           upper, lower, up_stage, down_stage, stage, part0, part, landed0, landed, gram0, cross,
           diag, diag_stage, gram, narrow, narrow_rest, square, square_rest, rotation,
           in_sem, out_sem, rs_send, rs_recv, ag_send, ag_recv, mv_send, mv_recv,
           dg_send, dg_recv, df_send, df_recv):
    f, r = lax.axis_index("factor"), lax.axis_index("rows")
    y = lax.rem(r, Y_SIZE)
    z_base = r - y
    height, half = upper.shape[1], upper.shape[2]
    width = 2 * half
    tall = height // CHUNKS
    above, below = lax.rem(f + 1, n_factor), lax.rem(f + n_factor - 1, n_factor)
    first, last = f == 0, f == n_factor - 1

    def peer(k):
        return lax.rem(r + k, n_rows)

    def peer_back(k):
        return lax.rem(r + n_rows - k, n_rows)

    load_u = pltpu.make_async_copy(working.at[:, pl.ds(0, half)], upper.at[0], in_sem.at[0])
    load_l = pltpu.make_async_copy(working.at[:, pl.ds(half, half)], lower.at[0], in_sem.at[1])
    load_u.start()
    load_l.start()
    barrier = pltpu.get_barrier_semaphore()
    for k in range(1, n_rows):
        pl.semaphore_signal(barrier, inc=1, device_id={"rows": peer(k)}, device_id_type=MESH)
    pl.semaphore_signal(barrier, inc=1, device_id={"factor": above}, device_id_type=MESH)
    pl.semaphore_signal(barrier, inc=1, device_id={"factor": below}, device_id_type=MESH)

    pending = []

    def reduce_rows(s, mine, landing, total):
        q = mine.shape[0] // n_rows

        def rows_of(device):
            return pl.ds(pl.multiple_of(device * q, q), q)

        def scatter(k):
            return remote(mine.at[rows_of(peer(k))], landing.at[k - 1],
                          rs_send.at[s, k], rs_recv.at[s, k], rows=peer(k))

        def gather(k, device):
            return remote(total.at[rows_of(device)], total.at[rows_of(device)],
                          ag_send.at[s, k], ag_recv.at[s, k], rows=peer(k))

        for k in range(1, n_rows):
            scatter(k).start()
        acc = mine[rows_of(r), :].astype(F32)
        for k in range(1, n_rows):
            scatter(k).wait_recv()
            acc = acc + landing[k - 1].astype(F32)
        total[rows_of(r), :] = acc.astype(total.dtype)
        for k in range(1, n_rows):
            gather(k, r).start()
        for k in range(1, n_rows):
            gather(k, peer_back(k)).wait_recv()
        pending.extend(functools.partial(scatter, k) for k in range(1, n_rows))
        pending.extend(functools.partial(gather, k, r) for k in range(1, n_rows))

    def solve(s):
        spectrum = 1.0 + levels[s].astype(F32) / float(width)
        squared = spectrum * spectrum
        norms = jnp.zeros((1, width), F32)
        for i in range(0, width, half):
            high = narrow[i:i + half, :]
            product = mm(high, narrow[...]) + mm(high, narrow_rest[...]) + mm(narrow_rest[i:i + half, :], narrow[...])
            square[i:i + half, :], square_rest[i:i + half, :] = halves(product)
            wide = gram[i:i + half, :]
            norms = norms + jnp.sum(wide * wide, axis=0, keepdims=True)
        total = jnp.sum(norms * squared, axis=1, keepdims=True)
        scale = (0.5 * math.sqrt(width)) / jnp.sqrt(total + 1e-06)
        outer = scale * spectrum
        cubic = (0.5 * scale * scale)
        for i in range(0, width, half):
            wide = gram[i:i + half, :]
            high, low = halves(wide * squared)
            third = mm(high, square[...]) + mm(high, square_rest[...]) + mm(low, square[...])
            rotation[i:i + half, :] = (outer * (1.5 * wide - cubic * third)).astype(BF16)

    def apply(s, c):
        rows = pl.ds(c * tall, tall)
        return mm(upper[s, rows, :], rotation[:half, :]) + mm(lower[s, rows, :], rotation[half:, :])

    def diag_slice(s, b, j):
        return diag.at[s, b, pl.ds(pl.multiple_of(j * (half // Y_SIZE), half // Y_SIZE), half // Y_SIZE)]

    def move_up(s, c):
        rows = pl.ds(c * tall, tall)
        return remote(up_stage.at[s, rows], upper.at[s + 1, rows], mv_send.at[s, 0, c], mv_recv.at[s, 0, c], factor=above)

    def move_down(s, c):
        rows = pl.ds(c * tall, tall)
        return remote(down_stage.at[s, rows], lower.at[s + 1, rows], mv_send.at[s, 1, c], mv_recv.at[s, 1, c], factor=below)

    def diag_up(s):
        own = pl.ds(pl.multiple_of(y * (half // Y_SIZE), half // Y_SIZE), half // Y_SIZE)
        return remote(diag_stage.at[s, 0, own], diag_slice(s, 0, y), dg_send.at[s, 0], dg_recv.at[s, 0], factor=above)

    def diag_down(s):
        own = pl.ds(pl.multiple_of(y * (half // Y_SIZE), half // Y_SIZE), half // Y_SIZE)
        return remote(diag_stage.at[s, 1, own], diag_slice(s, 1, y), dg_send.at[s, 1], dg_recv.at[s, 1], factor=below)

    def diag_spread(s, b, k, j):
        return remote(diag_slice(s, b, j), diag_slice(s, b, j), df_send.at[s, b, k], df_recv.at[s, b, k],
                      rows=z_base + lax.rem(y + k, Y_SIZE))

    def shift(s):
        for c in range(CHUNKS):
            rows = pl.ds(c * tall, tall)
            moved = apply(s, c)
            new_u, new_l = moved[:, :half], moved[:, half:]
            up_stage[s, rows, :] = jnp.where(first, new_l, new_u).astype(BF16)
            down_stage[s, rows, :] = new_l.astype(BF16)

            @pl.when(first)
            def _():
                upper[s + 1, rows, :] = new_u.astype(BF16)

            @pl.when(last)
            def _():
                lower[s + 1, rows, :] = new_u.astype(BF16)

            @pl.when(jnp.logical_not(last))
            def _():
                move_up(s, c).start()

            @pl.when(jnp.logical_not(first))
            def _():
                move_down(s, c).start()

            if c == 0:
                turned = mm(narrow[...], rotation[...]) + mm(narrow_rest[...], rotation[...])
                high, low = halves(turned)
                own_u = inner_rows(rotation[:, :half], high[:, :half]) + inner_rows(rotation[:, :half], low[:, :half])
                own_l = inner_rows(rotation[:, half:], high[:, half:]) + inner_rows(rotation[:, half:], low[:, half:])
                diag_stage[s, 0] = jnp.where(first, own_l, own_u)
                diag_stage[s, 1] = own_l
                diag_stage[s, 2] = own_u
                own = pl.ds(pl.multiple_of(y * (half // Y_SIZE), half // Y_SIZE), half // Y_SIZE)

                @pl.when(first)
                def _():
                    diag[s, 0, own, :] = diag_stage[s, 2, own, :]

                @pl.when(last)
                def _():
                    diag[s, 1, own, :] = diag_stage[s, 2, own, :]

                @pl.when(jnp.logical_not(last))
                def _():
                    diag_up(s).start()

                @pl.when(jnp.logical_not(first))
                def _():
                    diag_down(s).start()

        @pl.when(jnp.logical_not(first))
        def _():
            diag_up(s).wait_recv()

        for k in range(1, Y_SIZE):
            diag_spread(s, 0, k, y).start()

        @pl.when(jnp.logical_not(last))
        def _():
            diag_down(s).wait_recv()

        for k in range(1, Y_SIZE):
            diag_spread(s, 1, k, y).start()

        total = None
        for c in range(CHUNKS):
            rows = pl.ds(c * tall, tall)

            @pl.when(jnp.logical_not(first))
            def _():
                move_up(s, c).wait_recv()

            @pl.when(jnp.logical_not(last))
            def _():
                move_down(s, c).wait_recv()

            term = inner_rows(upper[s + 1, rows, :], lower[s + 1, rows, :])
            total = term if total is None else total + term
        part[s] = total.astype(BF16)

    load_u.wait()
    load_l.wait()
    part0[:half, :] = inner_rows(upper[0], upper[0]).astype(BF16)
    part0[half:width, :] = inner_rows(upper[0], lower[0]).astype(BF16)
    part0[width:, :] = inner_rows(lower[0], lower[0]).astype(BF16)
    pl.semaphore_wait(barrier, n_rows + 1)

    for s in range(steps):
        if s == 0:
            reduce_rows(s, part0, landed0, gram0)
            own_u, own_x, own_l = gram0[:half, :], gram0[half:width, :], gram0[width:, :]
        else:
            reduce_rows(s, part.at[s - 1], landed.at[s - 1], cross.at[s - 1])
            for b in range(2):
                for k in range(1, Y_SIZE):
                    diag_spread(s - 1, b, k, lax.rem(y + Y_SIZE - k, Y_SIZE)).wait_recv()
            own_u, own_x, own_l = diag[s - 1, 0], cross[s - 1], diag[s - 1, 1]
        gram[:half, :half] = own_u
        own_x = own_x.astype(F32)
        gram[:half, half:] = own_x
        gram[half:, :half] = own_x.T
        gram[half:, half:] = own_l
        narrow[...], narrow_rest[...] = halves(gram[...])
        solve(s)
        if s + 1 < steps:
            shift(s)

    stores = []
    for c in range(CHUNKS):
        rows = pl.ds(c * tall, tall)
        stage[rows, :] = apply(steps - 1, c).astype(BF16)
        store = pltpu.make_async_copy(stage.at[rows], out.at[rows], out_sem.at[c])
        store.start()
        stores.append(store)

    for copy in pending:
        copy().wait_send()
    for s in range(steps - 1):
        for c in range(CHUNKS):
            @pl.when(jnp.logical_not(last))
            def _():
                move_up(s, c).wait_send()

            @pl.when(jnp.logical_not(first))
            def _():
                move_down(s, c).wait_send()

        @pl.when(jnp.logical_not(last))
        def _():
            diag_up(s).wait_send()

        @pl.when(jnp.logical_not(first))
        def _():
            diag_down(s).wait_send()

        for b in range(2):
            for k in range(1, Y_SIZE):
                diag_spread(s, b, k, y).wait_send()
    for store in stores:
        store.wait()


def body(working, levels):
    height, width = working.shape
    half = width // 2
    steps = levels.shape[0]
    n_factor, n_rows = lax.axis_size("factor"), lax.axis_size("rows")
    dma = pltpu.SemaphoreType.DMA
    moves = steps - 1
    return pl.pallas_call(
        functools.partial(kernel, n_factor, n_rows, steps),
        out_shape=jax.ShapeDtypeStruct((height, width), BF16),
        in_specs=[pl.BlockSpec(memory_space=pl.ANY), pl.BlockSpec(memory_space=pltpu.VMEM)],
        out_specs=pl.BlockSpec(memory_space=pl.ANY),
        scratch_shapes=[
            pltpu.VMEM((steps, height, half), BF16),
            pltpu.VMEM((steps, height, half), BF16),
            pltpu.VMEM((moves, height, half), BF16),
            pltpu.VMEM((moves, height, half), BF16),
            pltpu.VMEM((height, width), BF16),
            pltpu.VMEM((3 * half, half), BF16),
            pltpu.VMEM((moves, half, half), BF16),
            pltpu.VMEM((n_rows - 1, 3 * half // n_rows, half), BF16),
            pltpu.VMEM((moves, n_rows - 1, half // n_rows, half), BF16),
            pltpu.VMEM((3 * half, half), F32),
            pltpu.VMEM((moves, half, half), BF16),
            pltpu.VMEM((moves, 2, half, half), F32),
            pltpu.VMEM((moves, 3, half, half), F32),
            pltpu.VMEM((width, width), F32),
            pltpu.VMEM((width, width), BF16),
            pltpu.VMEM((width, width), BF16),
            pltpu.VMEM((width, width), BF16),
            pltpu.VMEM((width, width), BF16),
            pltpu.VMEM((width, width), BF16),
            dma((2,)),
            dma((CHUNKS,)),
            dma((steps, n_rows)),
            dma((steps, n_rows)),
            dma((steps, n_rows)),
            dma((steps, n_rows)),
            dma((moves, 2, CHUNKS)),
            dma((moves, 2, CHUNKS)),
            dma((moves, 2)),
            dma((moves, 2)),
            dma((moves, 2, Y_SIZE)),
            dma((moves, 2, Y_SIZE)),
        ],
        compiler_params=pltpu.CompilerParams(
            collective_id=0, has_side_effects=True, vmem_limit_bytes=40 << 20
        ),
        cost_estimate=pl.CostEstimate(
            flops=steps * 4 * height * width * width, bytes_accessed=4 * height * width, transcendentals=0
        ),
        name="jacobi",
    )(working, levels)


def solution(mesh):
    placed = (P("rows", "factor"), P(None, "factor", None))
    return jax.shard_map(
        body, mesh=mesh, in_specs=placed, out_specs=P("rows", "factor"), check_vma=False
    )
```

time: 622 us -> 138 us (0.22)
  the two profiles are of different devices: /device:TPU:1 before, /device:TPU:129 now
where the time goes in v1:
time: 138 us
  Pallas kernels  135 us (98%)
  local copies, waits for them, and re-layouts  2.89 us (2%)
    pallas_call x1, Pallas kernels, body(): pl.pallas_call(functools.partial(kernel, n_factor, n_rows, steps), out_sh...  135 us
    unnamed x5, local copies, waits for them, and re-layouts  2.89 us

profile of v1, /device:TPU:129, one launch (start us, length us, event | category | flops | bytes accessed | tf_op | source)
XLA Modules:
  0.0 137.5 jit_solution(7875712669185702708)
XLA Ops:
  0.0 0.0 copy-start
  0.0 1.2 copy-done
  1.2 0.0 copy-start.1
  1.2 0.7 copy-done.1
  1.9 134.6 %jacobi.1 = bf16[1024,512]{1,0:T(8,128)(2,1)S(1)} custom-call(bf16[1024,512]{1,0:T(8,128)(2,1)S(1)} %copy-done, s32[3,1,512]{2,1,0:T(1,128)S(1)} %copy-done.1), custom_call_target="tpu_custom_call" | custom-call | flops 3221225472 | bytes 2097152 | tf_op jit(solution)/shard_map/jacobi/pallas_call | solution.py:294
  136.6 1.0 copy.4
Async XLA Ops:
  0.0 1.2 copy-start
  1.2 0.7 copy-start.1

commit v2 on v0

v2 whole, which is shorter than its diff:
```python
import functools
import math

import jax
import jax.numpy as jnp
from jax import lax
from jax.experimental import pallas as pl
from jax.experimental.pallas import tpu as pltpu
from jax.sharding import PartitionSpec as P

MESH = pl.DeviceIdType.MESH
F32, BF16 = jnp.float32, jnp.bfloat16
Y_SIZE = 4
CHUNKS = 4


def inner_rows(left, right):
    return lax.dot_general(
        left, right, (((0,), (0,)), ((), ())), preferred_element_type=F32
    )


def mm(left, right):
    return jnp.dot(left, right, preferred_element_type=F32)


def halves(wide):
    high = wide.astype(BF16)
    return high, (wide - high.astype(F32)).astype(BF16)


def remote(src, dst, send, recv, **to):
    return pltpu.make_async_remote_copy(
        src_ref=src, dst_ref=dst, send_sem=send, recv_sem=recv, device_id=to, device_id_type=MESH
    )


def kernel(n_factor, n_rows, steps, working, levels_in, out,
           levels, blocks, outs, part0, part, landed0, landed, gram0, cross,
           own_squares, squares, diag, diag_stage, gram, narrow, narrow_rest, square, square_rest, rotation,
           in_sem, sq_send, sq_recv, rs_send, rs_recv, ag_send, ag_recv, agz_send, agz_recv, agy_send, agy_recv, mv_send, mv_recv,
           dg_send, dg_recv, df_send, df_recv):
    f, r = lax.axis_index("factor"), lax.axis_index("rows")
    y = lax.rem(r, Y_SIZE)
    z = r // Y_SIZE
    z_size = n_rows // Y_SIZE
    height, half = blocks.shape[2], blocks.shape[3]
    width = 2 * half
    tall = height // CHUNKS
    above, below = lax.rem(f + 1, n_factor), lax.rem(f + n_factor - 1, n_factor)
    first, last = f == 0, f == n_factor - 1
    not_first, not_last = f > 0, f < n_factor - 1

    def peer(k):
        return lax.rem(r + k, n_rows)

    def peer_back(k):
        return lax.rem(r + n_rows - k, n_rows)

    loads = [pltpu.make_async_copy(working.at[:, pl.ds(b * half, half)], blocks.at[0, b], in_sem.at[b]) for b in range(2)]
    loads.append(pltpu.make_async_copy(levels_in, levels, in_sem.at[2]))
    for load in loads:
        load.start()
    barrier = pltpu.get_barrier_semaphore()
    for k in range(1, n_rows):
        pl.semaphore_signal(barrier, inc=1, device_id={"rows": peer(k)}, device_id_type=MESH)
    for to in (above, below):
        pl.semaphore_signal(barrier, inc=1, device_id={"factor": to}, device_id_type=MESH)

    sent = []

    def start(copy, when=None):
        if when is None:
            copy().start()
        else:
            @pl.when(when)
            def _():
                copy().start()
        sent.append((copy, when))

    def landed_on(copy, when=None):
        if when is None:
            copy().wait_recv()
        else:
            @pl.when(when)
            def _():
                copy().wait_recv()

    def scatter_rows(s, mine, landing, meanwhile=None):
        q = mine.shape[0] // n_rows

        def rows_of(device):
            return pl.ds(pl.multiple_of(device * q, q), q)

        def scatter(k):
            return remote(mine.at[rows_of(peer(k))], landing.at[k - 1],
                          rs_send.at[s, k], rs_recv.at[s, k], rows=peer(k))

        for k in range(1, n_rows):
            start(functools.partial(scatter, k))
        if meanwhile is not None:
            meanwhile()
        acc = mine[rows_of(r), :].astype(F32)
        for k in range(1, n_rows):
            scatter(k).wait_recv()
            acc = acc + landing[k - 1].astype(F32)
        return acc, rows_of

    def gather_rows(s, acc, rows_of, total):
        def gather(k, device):
            return remote(total.at[rows_of(device)], total.at[rows_of(device)],
                          ag_send.at[s, k], ag_recv.at[s, k], rows=peer(k))

        total[rows_of(r), :] = acc.astype(total.dtype)
        for k in range(1, n_rows):
            start(functools.partial(gather, k, r))
        for k in range(1, n_rows):
            gather(k, peer_back(k)).wait_recv()

    def gather_rows_by_axes(s, acc, rows_of, total):
        def along_z(k, device):
            return remote(total.at[rows_of(device)], total.at[rows_of(device)], agz_send.at[s, k], agz_recv.at[s, k],
                          rows=lax.rem(z + k, z_size) * Y_SIZE + y)

        def along_y(k, j, device):
            return remote(total.at[rows_of(device)], total.at[rows_of(device)], agy_send.at[s, k, j], agy_recv.at[s, k, j],
                          rows=z * Y_SIZE + lax.rem(y + j, Y_SIZE))

        def at(k, j):
            return lax.rem(z + z_size - k, z_size) * Y_SIZE + lax.rem(y + Y_SIZE - j, Y_SIZE)

        total[rows_of(r), :] = acc.astype(total.dtype)
        for k in range(1, z_size):
            start(functools.partial(along_z, k, r))
        for k in range(z_size):
            if k:
                along_z(k, at(k, 0)).wait_recv()
            for j in range(1, Y_SIZE):
                start(functools.partial(along_y, k, j, at(k, 0)))
        for k in range(z_size):
            for j in range(1, Y_SIZE):
                along_y(k, j, at(k, j)).wait_recv()

    def solve(s):
        spectrum = 1.0 + levels[s].astype(F32) / float(width)
        squared = spectrum * spectrum
        norms = jnp.zeros((1, width), F32)
        for i in range(0, width, half):
            high = narrow[i:i + half, :]
            product = mm(high, narrow[...]) + mm(high, narrow_rest[...]) + mm(narrow_rest[i:i + half, :], narrow[...])
            square[i:i + half, :], square_rest[i:i + half, :] = halves(product)
            wide = gram[i:i + half, :]
            norms = norms + jnp.sum(wide * wide, axis=0, keepdims=True)
        total = jnp.sum(norms * squared, axis=1, keepdims=True)
        scale = (0.5 * math.sqrt(width)) / jnp.sqrt(total + 1e-06)
        outer = scale * spectrum
        cubic = (0.5 * scale * scale)
        for i in range(0, width, half):
            wide = gram[i:i + half, :]
            high, low = halves(wide * squared)
            third = mm(high, square[...]) + mm(high, square_rest[...]) + mm(low, square[...])
            result = (outer * (1.5 * wide - cubic * third)).astype(BF16)
            rotation[s, 0, i:i + half, :] = result[:, :half]
            rotation[s, 1, i:i + half, :] = result[:, half:]

    def apply(s, rows, b):
        return mm(blocks[s, 0, rows, :], rotation[s, b, :half, :]) + mm(blocks[s, 1, rows, :], rotation[s, b, half:, :])

    quarter = half // Y_SIZE

    def quarter_of(j):
        return pl.ds(pl.multiple_of(j * quarter, quarter), quarter)

    def diag_move(s, b):
        return remote(diag_stage.at[s, b, quarter_of(y)], diag.at[s, b, quarter_of(y)],
                      dg_send.at[s, b], dg_recv.at[s, b], factor=above if b == 0 else below)

    def diag_spread(s, b, k, j):
        return remote(diag.at[s, b, quarter_of(j)], diag.at[s, b, quarter_of(j)], df_send.at[s, b, k], df_recv.at[s, b, k],
                      rows=z * Y_SIZE + lax.rem(y + k, Y_SIZE))

    def send_diag(s):
        turned = []
        for b in range(2):
            turned.append(halves(mm(narrow[...], rotation[s, b]) + mm(narrow_rest[...], rotation[s, b])))
        own_u, own_l = (inner_rows(rotation[s, b], turned[b][0]) + inner_rows(rotation[s, b], turned[b][1]) for b in range(2))
        diag_stage[s, 0] = jnp.where(first, own_l, own_u)
        diag_stage[s, 1] = own_l
        diag_stage[s, 2] = own_u

        @pl.when(first)
        def _():
            diag[s, 0, quarter_of(y), :] = diag_stage[s, 2, quarter_of(y), :]

        @pl.when(last)
        def _():
            diag[s, 1, quarter_of(y), :] = diag_stage[s, 2, quarter_of(y), :]

        start(functools.partial(diag_move, s, 0), not_last)
        start(functools.partial(diag_move, s, 1), not_first)

    def spread_diag(s):
        for b in range(2):
            landed_on(functools.partial(diag_move, s, b), not_first if b == 0 else not_last)
            for k in range(1, Y_SIZE):
                start(functools.partial(diag_spread, s, b, k, y))

    def chunk(c):
        return pl.ds(c * tall, tall)

    def move(s, c, b):
        return remote(outs.at[s, b, chunk(c)], blocks.at[s + 1, b, chunk(c)], mv_send.at[s, b, c], mv_recv.at[s, b, c],
                      factor=above if b == 0 else below)

    def rotate_and_send(s):
        for c in range(CHUNKS):
            new_u, new_l = apply(s, chunk(c), 0), apply(s, chunk(c), 1)
            outs[s, 0, chunk(c), :] = jnp.where(first, new_l, new_u).astype(BF16)
            outs[s, 1, chunk(c), :] = new_l.astype(BF16)

            @pl.when(first)
            def _():
                blocks[s + 1, 0, chunk(c), :] = new_u.astype(BF16)

            @pl.when(last)
            def _():
                blocks[s + 1, 1, chunk(c), :] = new_u.astype(BF16)

            start(functools.partial(move, s, c, 0), not_last)
            start(functools.partial(move, s, c, 1), not_first)
        send_diag(s)

    def cross_of(s):
        total = None
        for c in range(CHUNKS):
            landed_on(functools.partial(move, s - 1, c, 0), not_first)
            landed_on(functools.partial(move, s - 1, c, 1), not_last)
            term = inner_rows(blocks[s, 0, chunk(c), :], blocks[s, 1, chunk(c), :])
            total = term if total is None else total + term
        return total

    def back(k):
        return lax.rem(y + Y_SIZE - k, Y_SIZE)

    def finish_gram(s, own_x):
        for b in range(2):
            for k in range(1, Y_SIZE):
                diag_spread(s, b, k, back(k)).wait_recv()
        own_x = own_x.astype(F32)
        gram[:half, :half] = diag[s, 0]
        gram[:half, half:] = own_x
        gram[half:, :half] = own_x.T
        gram[half:, half:] = diag[s, 1]
        narrow[...], narrow_rest[...] = halves(gram[...])

    for load in loads:
        load.wait()
    tile = half // 2
    corners = [(0, 0), (0, 1), (1, 1)]
    every = [(0, 0), (0, 1), (1, 0), (1, 1)]
    spots = [(0, 0, c) for c in corners] + [(0, 1, c) for c in every] + [(1, 1, c) for c in corners]
    products = {(a, b): inner_rows(blocks[0, a], blocks[0, b]).astype(BF16) for a, b in ((0, 0), (0, 1), (1, 1))}
    for n, (a, b, (i, j)) in enumerate(spots):
        part0[n * tile:(n + 1) * tile, :] = products[a, b][i * tile:(i + 1) * tile, j * tile:(j + 1) * tile]
    pl.semaphore_wait(barrier, n_rows + 1)
    own_squares[...] = jnp.zeros_like(own_squares)
    for b in range(2):
        wide = blocks[0, b].astype(F32)
        sums = jnp.sum(wide * wide, axis=0, keepdims=True)
        for i in range(2):
            own_squares[2 * b + i:2 * b + i + 1, :] = sums[:, i * tile:(i + 1) * tile]

    def spread_squares(k):
        return remote(own_squares, squares.at[k - 1], sq_send.at[k], sq_recv.at[k], rows=peer(k))

    def send_squares():
        for k in range(1, n_rows):
            start(functools.partial(spread_squares, k))

    acc, rows_of = scatter_rows(0, part0, landed0, send_squares)
    gather_rows_by_axes(0, acc, rows_of, gram0)
    for n, (a, b, (i, j)) in enumerate(spots):
        row, col = a * half + i * tile, b * half + j * tile
        piece = gram0[n * tile:(n + 1) * tile, :]
        gram[row:row + tile, col:col + tile] = piece
        if row != col:
            gram[col:col + tile, row:row + tile] = piece.T
    sums = own_squares[...]
    for k in range(1, n_rows):
        spread_squares(k).wait_recv()
        sums = sums + squares[k - 1]
    on_diagonal = lax.broadcasted_iota(jnp.int32, (tile, tile), 0) == lax.broadcasted_iota(jnp.int32, (tile, tile), 1)
    for i in range(2 * half // tile):
        at = slice(i * tile, (i + 1) * tile)
        gram[at, at] = jnp.where(on_diagonal, sums[i:i + 1, :], gram[at, at])
    narrow[...], narrow_rest[...] = halves(gram[...])
    solve(0)
    rotate_and_send(0)

    part[0] = cross_of(1).astype(BF16)
    acc, rows_of = scatter_rows(1, part.at[0], landed.at[0], lambda: spread_diag(0))
    gather_rows(0, acc, rows_of, cross.at[0])
    finish_gram(0, cross[0])
    solve(1)
    rotate_and_send(1)

    part[1] = cross_of(2).astype(BF16)
    acc, rows_of = scatter_rows(2, part.at[1], landed.at[1], lambda: spread_diag(1))
    gather_rows(1, acc, rows_of, cross.at[1])
    finish_gram(1, cross[1])
    solve(2)
    for c in range(CHUNKS):
        for b in range(2):
            out[chunk(c), b * half:(b + 1) * half] = apply(2, chunk(c), b).astype(BF16)

    for copy, when in sent:
        if when is None:
            copy().wait_send()
        else:
            @pl.when(when)
            def _():
                copy().wait_send()


def body(working, levels):
    height, width = working.shape
    half = width // 2
    steps = levels.shape[0]
    n_factor, n_rows = lax.axis_size("factor"), lax.axis_size("rows")
    dma = pltpu.SemaphoreType.DMA
    moves = steps - 1
    triangle = 10 * half // 2
    pairs = lambda *shape: [dma(shape), dma(shape)]
    return pl.pallas_call(
        functools.partial(kernel, n_factor, n_rows, steps),
        out_shape=jax.ShapeDtypeStruct((height, width), BF16),
        in_specs=[pl.BlockSpec(memory_space=pltpu.HBM), pl.BlockSpec(memory_space=pltpu.HBM)],
        out_specs=pl.BlockSpec(memory_space=pltpu.VMEM),
        scratch_shapes=[
            pltpu.VMEM(levels.shape, jnp.int32),
            pltpu.VMEM((steps, 2, height, half), BF16),
            pltpu.VMEM((moves, 2, height, half), BF16),
            pltpu.VMEM((triangle, half // 2), BF16),
            pltpu.VMEM((moves, half, half), BF16),
            pltpu.VMEM((n_rows - 1, triangle // n_rows, half // 2), BF16),
            pltpu.VMEM((moves, n_rows - 1, half // n_rows, half), BF16),
            pltpu.VMEM((triangle, half // 2), F32),
            pltpu.VMEM((moves, half, half), BF16),
            pltpu.VMEM((8, half // 2), F32),
            pltpu.VMEM((n_rows - 1, 8, half // 2), F32),
            pltpu.VMEM((moves, 2, half, half), F32),
            pltpu.VMEM((moves, 3, half, half), F32),
            pltpu.VMEM((width, width), F32),
            pltpu.VMEM((width, width), BF16),
            pltpu.VMEM((width, width), BF16),
            pltpu.VMEM((width, width), BF16),
            pltpu.VMEM((width, width), BF16),
            pltpu.VMEM((steps, 2, width, half), BF16),
            dma((3,)),
            *pairs(n_rows),
            *pairs(steps, n_rows),
            *pairs(moves, n_rows),
            *pairs(steps, n_rows // Y_SIZE),
            *pairs(steps, n_rows // Y_SIZE, Y_SIZE),
            *pairs(moves, 2, CHUNKS),
            *pairs(moves, 2),
            *pairs(moves, 2, Y_SIZE),
        ],
        compiler_params=pltpu.CompilerParams(
            collective_id=0, has_side_effects=True, vmem_limit_bytes=48 << 20
        ),
        cost_estimate=pl.CostEstimate(
            flops=steps * 4 * height * width * width, bytes_accessed=4 * height * width, transcendentals=0
        ),
        name="jacobi",
    )(working, levels)


def solution(mesh):
    placed = (P("rows", "factor"), P(None, "factor", None))
    return jax.shard_map(
        body, mesh=mesh, in_specs=placed, out_specs=P("rows", "factor"), check_vma=False
    )
```

time: 622 us -> 125 us (0.20); the launches traced: 613 us -> 125 us
  waiting for transfers between devices: 525 us -> 0 us
  Pallas kernels: 0 us -> 122 us
  starting transfers between devices: 40.7 us -> 0 us
  matrix products: 19.9 us -> 0 us
  between operations: 15.3 us -> 0.01 us
  other arithmetic: 8.94 us -> 0 us
    psum x3 -> x0, waiting for transfers between devices: 479 us -> none  [body(): gram = lax.psum(inner_rows(working, working), 'rows')]
    pallas_call x0 -> x1, Pallas kernels: none -> 122 us  [body(): pl.pallas_call(functools.partial(kernel, n_factor, n_rows, steps), out_sh...]
    ppermute x4 -> x0, waiting for transfers between devices: 46.1 us -> none  [passed_along(): return lax.ppermute(value, axis, pairs)]
    ppermute x4 -> x0, starting transfers between devices: 40.6 us -> none  [passed_along(): return lax.ppermute(value, axis, pairs)]
    dot_general x12 -> x0, matrix products: 19.9 us -> none  [the longest x3 5.82 us: body(): inner = jnp.dot(start.T, start, precision=lax.Precision.HIGHEST)]
    reduce_sum x3 -> x0, other arithmetic: 6.56 us -> none  [body(): frobenius = jnp.sqrt(jnp.sum(scaled * scaled) + 1e-06)]
  transfers between devices with their start and end apart: 7 -> 0, of which waited for: 7 -> 0; matrix products, arithmetic and copies ran while one was open for 0% -> 0% of each run, Pallas kernels for 0% -> 0%
where the time goes in v2:
time: 125 us
  Pallas kernels  122 us (98%)
  local copies, waits for them, and re-layouts  2.89 us (2%)
    pallas_call x1, Pallas kernels, body(): pl.pallas_call(functools.partial(kernel, n_factor, n_rows, steps), out_sh...  122 us
    unnamed x5, local copies, waits for them, and re-layouts  2.89 us

profile of v2, /device:TPU:1, one launch (start us, length us, event | category | flops | bytes accessed | tf_op | source)
XLA Modules:
  0.0 125.3 jit_solution(255327340954190741)
XLA Ops:
  0.0 0.0 copy-start
  0.0 1.2 copy-done
  1.2 0.0 copy-start.1
  1.2 0.7 copy-done.1
  1.9 122.4 %jacobi.1 = bf16[1024,512]{1,0:T(8,128)(2,1)S(1)} custom-call(bf16[1024,512]{1,0:T(8,128)(2,1)S(1)} %copy-done, s32[3,1,512]{2,1,0:T(1,128)S(1)} %copy-done.1), custom_call_target="tpu_custom_call" | custom-call | flops 3221225472 | bytes 2097152 | tf_op jit(solution)/shard_map/jacobi/pallas_call | solution.py:334
  124.3 1.0 copy.4
Async XLA Ops:
  0.0 1.2 copy-start
  1.2 0.7 copy-start.1

commit v3 on v2

--- a/solution.py
+++ b/solution.py
@@ -37,9 +37,9 @@
 
 def kernel(n_factor, n_rows, steps, working, levels_in, out,
            levels, blocks, outs, part0, part, landed0, landed, gram0, cross,
-           own_squares, squares, diag, diag_stage, gram, narrow, narrow_rest, square, square_rest, rotation,
+           own_squares, squares, diag, diag_stage, line, line_stage, gram, narrow, narrow_rest, square, square_rest, rotation,
            in_sem, sq_send, sq_recv, rs_send, rs_recv, ag_send, ag_recv, agz_send, agz_recv, agy_send, agy_recv, mv_send, mv_recv,
-           dg_send, dg_recv, df_send, df_recv):
+           dg_send, dg_recv, df_send, df_recv, ln_send, ln_recv):
     f, r = lax.axis_index("factor"), lax.axis_index("rows")
     y = lax.rem(r, Y_SIZE)
     z = r // Y_SIZE
@@ -67,6 +67,7 @@
     for to in (above, below):
         pl.semaphore_signal(barrier, inc=1, device_id={"factor": to}, device_id_type=MESH)
 
+    on_diagonal = lax.broadcasted_iota(jnp.int32, (half, half), 0) == lax.broadcasted_iota(jnp.int32, (half, half), 1)
     sent = []
 
     def start(copy, when=None):
@@ -146,22 +147,24 @@
         squared = spectrum * spectrum
         norms = jnp.zeros((1, width), F32)
         for i in range(0, width, half):
+            wide = gram[i:i + half, :] * spectrum
+            norms = norms + jnp.sum(wide * wide, axis=0, keepdims=True)
+        norm = jnp.sqrt(jnp.sum(norms, axis=1, keepdims=True) + 1e-06)
+        scale = (0.5 * math.sqrt(width)) / norm
+        for i in range(0, width, half):
+            narrow[i:i + half, :], narrow_rest[i:i + half, :] = halves(gram[i:i + half, :] * scale)
+        for i in range(0, width, half):
             high = narrow[i:i + half, :]
             product = mm(high, narrow[...]) + mm(high, narrow_rest[...]) + mm(narrow_rest[i:i + half, :], narrow[...])
             square[i:i + half, :], square_rest[i:i + half, :] = halves(product)
-            wide = gram[i:i + half, :]
-            norms = norms + jnp.sum(wide * wide, axis=0, keepdims=True)
-        total = jnp.sum(norms * squared, axis=1, keepdims=True)
-        scale = (0.5 * math.sqrt(width)) / jnp.sqrt(total + 1e-06)
-        outer = scale * spectrum
-        cubic = (0.5 * scale * scale)
         for i in range(0, width, half):
-            wide = gram[i:i + half, :]
+            wide = gram[i:i + half, :] * scale
             high, low = halves(wide * squared)
             third = mm(high, square[...]) + mm(high, square_rest[...]) + mm(low, square[...])
-            result = (outer * (1.5 * wide - cubic * third)).astype(BF16)
+            result = (spectrum * (1.5 * wide - 0.5 * third)).astype(BF16)
             rotation[s, 0, i:i + half, :] = result[:, :half]
             rotation[s, 1, i:i + half, :] = result[:, half:]
+        return norm / (0.5 * math.sqrt(width))
 
     def apply(s, rows, b):
         return mm(blocks[s, 0, rows, :], rotation[s, b, :half, :]) + mm(blocks[s, 1, rows, :], rotation[s, b, half:, :])
@@ -175,29 +178,39 @@
         return remote(diag_stage.at[s, b, quarter_of(y)], diag.at[s, b, quarter_of(y)],
                       dg_send.at[s, b], dg_recv.at[s, b], factor=above if b == 0 else below)
 
+    def line_move(s, b):
+        return remote(line_stage.at[s, b], line.at[s, b], ln_send.at[s, b], ln_recv.at[s, b], factor=above if b == 0 else below)
+
     def diag_spread(s, b, k, j):
         return remote(diag.at[s, b, quarter_of(j)], diag.at[s, b, quarter_of(j)], df_send.at[s, b, k], df_recv.at[s, b, k],
                       rows=z * Y_SIZE + lax.rem(y + k, Y_SIZE))
 
-    def send_diag(s):
+    def send_diag(s, size):
         turned = []
         for b in range(2):
             turned.append(halves(mm(narrow[...], rotation[s, b]) + mm(narrow_rest[...], rotation[s, b])))
-        own_u, own_l = (inner_rows(rotation[s, b], turned[b][0]) + inner_rows(rotation[s, b], turned[b][1]) for b in range(2))
-        diag_stage[s, 0] = jnp.where(first, own_l, own_u)
-        diag_stage[s, 1] = own_l
-        diag_stage[s, 2] = own_u
+        own_u, own_l = (size * (inner_rows(rotation[s, b], turned[b][0]) + inner_rows(rotation[s, b], turned[b][1]))
+                        for b in range(2))
+        line_u, line_l = (jnp.sum(jnp.where(on_diagonal, own, 0.0), axis=0, keepdims=True) for own in (own_u, own_l))
+        for i, (own, own_line) in enumerate(((jnp.where(first, own_l, own_u), jnp.where(first, line_l, line_u)),
+                                             (own_l, line_l), (own_u, line_u))):
+            diag_stage[s, i] = own.astype(BF16)
+            line_stage[s, i] = jnp.broadcast_to(own_line, (8, half))
 
         @pl.when(first)
         def _():
             diag[s, 0, quarter_of(y), :] = diag_stage[s, 2, quarter_of(y), :]
+            line[s, 0] = line_stage[s, 2]
 
         @pl.when(last)
         def _():
             diag[s, 1, quarter_of(y), :] = diag_stage[s, 2, quarter_of(y), :]
+            line[s, 1] = line_stage[s, 2]
 
         start(functools.partial(diag_move, s, 0), not_last)
         start(functools.partial(diag_move, s, 1), not_first)
+        start(functools.partial(line_move, s, 0), not_last)
+        start(functools.partial(line_move, s, 1), not_first)
 
     def spread_diag(s):
         for b in range(2):
@@ -212,7 +225,7 @@
         return remote(outs.at[s, b, chunk(c)], blocks.at[s + 1, b, chunk(c)], mv_send.at[s, b, c], mv_recv.at[s, b, c],
                       factor=above if b == 0 else below)
 
-    def rotate_and_send(s):
+    def rotate_and_send(s, size):
         for c in range(CHUNKS):
             new_u, new_l = apply(s, chunk(c), 0), apply(s, chunk(c), 1)
             outs[s, 0, chunk(c), :] = jnp.where(first, new_l, new_u).astype(BF16)
@@ -228,7 +241,7 @@
 
             start(functools.partial(move, s, c, 0), not_last)
             start(functools.partial(move, s, c, 1), not_first)
-        send_diag(s)
+        send_diag(s, size)
 
     def cross_of(s):
         total = None
@@ -246,12 +259,12 @@
         for b in range(2):
             for k in range(1, Y_SIZE):
                 diag_spread(s, b, k, back(k)).wait_recv()
+            landed_on(functools.partial(line_move, s, b), not_first if b == 0 else not_last)
+            at = slice(b * half, (b + 1) * half)
+            gram[at, at] = jnp.where(on_diagonal, line[s, b, 0:1, :], diag[s, b].astype(F32))
         own_x = own_x.astype(F32)
-        gram[:half, :half] = diag[s, 0]
         gram[:half, half:] = own_x
         gram[half:, :half] = own_x.T
-        gram[half:, half:] = diag[s, 1]
-        narrow[...], narrow_rest[...] = halves(gram[...])
 
     for load in loads:
         load.wait()
@@ -281,7 +294,7 @@
     gather_rows_by_axes(0, acc, rows_of, gram0)
     for n, (a, b, (i, j)) in enumerate(spots):
         row, col = a * half + i * tile, b * half + j * tile
-        piece = gram0[n * tile:(n + 1) * tile, :]
+        piece = gram0[n * tile:(n + 1) * tile, :].astype(F32)
         gram[row:row + tile, col:col + tile] = piece
         if row != col:
             gram[col:col + tile, row:row + tile] = piece.T
@@ -289,20 +302,17 @@
     for k in range(1, n_rows):
         spread_squares(k).wait_recv()
         sums = sums + squares[k - 1]
-    on_diagonal = lax.broadcasted_iota(jnp.int32, (tile, tile), 0) == lax.broadcasted_iota(jnp.int32, (tile, tile), 1)
     for i in range(2 * half // tile):
         at = slice(i * tile, (i + 1) * tile)
-        gram[at, at] = jnp.where(on_diagonal, sums[i:i + 1, :], gram[at, at])
-    narrow[...], narrow_rest[...] = halves(gram[...])
-    solve(0)
-    rotate_and_send(0)
+        gram[at, at] = jnp.where(on_diagonal[:tile, :tile], sums[i:i + 1, :], gram[at, at])
+    size = solve(0)
+    rotate_and_send(0, size)
 
     part[0] = cross_of(1).astype(BF16)
     acc, rows_of = scatter_rows(1, part.at[0], landed.at[0], lambda: spread_diag(0))
     gather_rows(0, acc, rows_of, cross.at[0])
     finish_gram(0, cross[0])
-    solve(1)
-    rotate_and_send(1)
+    rotate_and_send(1, solve(1))
 
     part[1] = cross_of(2).astype(BF16)
     acc, rows_of = scatter_rows(2, part.at[1], landed.at[1], lambda: spread_diag(1))
@@ -344,12 +354,14 @@
             pltpu.VMEM((moves, half, half), BF16),
             pltpu.VMEM((n_rows - 1, triangle // n_rows, half // 2), BF16),
             pltpu.VMEM((moves, n_rows - 1, half // n_rows, half), BF16),
-            pltpu.VMEM((triangle, half // 2), F32),
+            pltpu.VMEM((triangle, half // 2), BF16),
             pltpu.VMEM((moves, half, half), BF16),
             pltpu.VMEM((8, half // 2), F32),
             pltpu.VMEM((n_rows - 1, 8, half // 2), F32),
-            pltpu.VMEM((moves, 2, half, half), F32),
-            pltpu.VMEM((moves, 3, half, half), F32),
+            pltpu.VMEM((moves, 2, half, half), BF16),
+            pltpu.VMEM((moves, 3, half, half), BF16),
+            pltpu.VMEM((moves, 2, 8, half), F32),
+            pltpu.VMEM((moves, 3, 8, half), F32),
             pltpu.VMEM((width, width), F32),
             pltpu.VMEM((width, width), BF16),
             pltpu.VMEM((width, width), BF16),
@@ -365,9 +377,10 @@
             *pairs(moves, 2, CHUNKS),
             *pairs(moves, 2),
             *pairs(moves, 2, Y_SIZE),
+            *pairs(moves, 2),
         ],
         compiler_params=pltpu.CompilerParams(
-            collective_id=0, has_side_effects=True, vmem_limit_bytes=48 << 20
+            collective_id=0, has_side_effects=True, vmem_limit_bytes=52 << 20
         ),
         cost_estimate=pl.CostEstimate(
             flops=steps * 4 * height * width * width, bytes_accessed=4 * height * width, transcendentals=0

time: 125 us -> 122 us (0.976)
  Pallas kernels: 122 us -> 120 us
    pallas_call x1, Pallas kernels: 122 us -> 120 us  [body(): pl.pallas_call(functools.partial(kernel, n_factor, n_rows, steps), out_sh...]
    unnamed x5 -> x3, local copies, waits for them, and re-layouts: 2.89 us -> 1.66 us
where the time goes in v3:
time: 122 us
  Pallas kernels  120 us (98%)
  local copies, waits for them, and re-layouts  1.66 us (1%)
    pallas_call x1, Pallas kernels, body(): pl.pallas_call(functools.partial(kernel, n_factor, n_rows, steps), out_sh...  120 us

profile of v3, /device:TPU:1, one launch (start us, length us, event | category | flops | bytes accessed | tf_op | source)
XLA Modules:
  0.0 121.9 jit_solution(17004015332465423759)
XLA Ops:
  0.0 0.0 copy-start
  0.0 0.7 copy-done
  0.7 120.2 %jacobi.1 = bf16[1024,512]{1,0:T(8,128)(2,1)S(1)} custom-call(bf16[1024,512]{1,0:T(8,128)(2,1)} %working.1, s32[3,1,512]{2,1,0:T(1,128)S(1)} %copy-done), custom_call_target="tpu_custom_call" | custom-call | flops 3221225472 | bytes 2097152 | tf_op jit(solution)/shard_map/jacobi/pallas_call | solution.py:344
  120.9 1.0 copy.4
Async XLA Ops:
  0.0 0.7 copy-start

commit v4 on v3

--- a/solution.py
+++ b/solution.py
@@ -38,7 +38,7 @@
 def kernel(n_factor, n_rows, steps, working, levels_in, out,
            levels, blocks, outs, part0, part, landed0, landed, gram0, cross,
            own_squares, squares, diag, diag_stage, line, line_stage, gram, narrow, narrow_rest, square, square_rest, rotation,
-           in_sem, sq_send, sq_recv, rs_send, rs_recv, ag_send, ag_recv, agz_send, agz_recv, agy_send, agy_recv, mv_send, mv_recv,
+           in_sem, sq_send, sq_recv, rs_send, rs_recv, agz_send, agz_recv, agy_send, agy_recv, mv_send, mv_recv,
            dg_send, dg_recv, df_send, df_recv, ln_send, ln_recv):
     f, r = lax.axis_index("factor"), lax.axis_index("rows")
     y = lax.rem(r, Y_SIZE)
@@ -107,18 +107,7 @@
             acc = acc + landing[k - 1].astype(F32)
         return acc, rows_of
 
-    def gather_rows(s, acc, rows_of, total):
-        def gather(k, device):
-            return remote(total.at[rows_of(device)], total.at[rows_of(device)],
-                          ag_send.at[s, k], ag_recv.at[s, k], rows=peer(k))
-
-        total[rows_of(r), :] = acc.astype(total.dtype)
-        for k in range(1, n_rows):
-            start(functools.partial(gather, k, r))
-        for k in range(1, n_rows):
-            gather(k, peer_back(k)).wait_recv()
-
-    def gather_rows_by_axes(s, acc, rows_of, total):
+    def gather_rows(s, acc, rows_of, total, meanwhile):
         def along_z(k, device):
             return remote(total.at[rows_of(device)], total.at[rows_of(device)], agz_send.at[s, k], agz_recv.at[s, k],
                           rows=lax.rem(z + k, z_size) * Y_SIZE + y)
@@ -138,6 +127,7 @@
                 along_z(k, at(k, 0)).wait_recv()
             for j in range(1, Y_SIZE):
                 start(functools.partial(along_y, k, j, at(k, 0)))
+        meanwhile()
         for k in range(z_size):
             for j in range(1, Y_SIZE):
                 along_y(k, j, at(k, j)).wait_recv()
@@ -185,7 +175,7 @@
         return remote(diag.at[s, b, quarter_of(j)], diag.at[s, b, quarter_of(j)], df_send.at[s, b, k], df_recv.at[s, b, k],
                       rows=z * Y_SIZE + lax.rem(y + k, Y_SIZE))
 
-    def send_diag(s, size):
+    def make_diag(s, size):
         turned = []
         for b in range(2):
             turned.append(halves(mm(narrow[...], rotation[s, b]) + mm(narrow_rest[...], rotation[s, b])))
@@ -207,10 +197,10 @@
             diag[s, 1, quarter_of(y), :] = diag_stage[s, 2, quarter_of(y), :]
             line[s, 1] = line_stage[s, 2]
 
-        start(functools.partial(diag_move, s, 0), not_last)
-        start(functools.partial(diag_move, s, 1), not_first)
-        start(functools.partial(line_move, s, 0), not_last)
-        start(functools.partial(line_move, s, 1), not_first)
+    def send_diag(s):
+        for moved in (diag_move, line_move):
+            start(functools.partial(moved, s, 0), not_last)
+            start(functools.partial(moved, s, 1), not_first)
 
     def spread_diag(s):
         for b in range(2):
@@ -241,7 +231,7 @@
 
             start(functools.partial(move, s, c, 0), not_last)
             start(functools.partial(move, s, c, 1), not_first)
-        send_diag(s, size)
+        make_diag(s, size)
 
     def cross_of(s):
         total = None
@@ -276,22 +266,21 @@
     for n, (a, b, (i, j)) in enumerate(spots):
         part0[n * tile:(n + 1) * tile, :] = products[a, b][i * tile:(i + 1) * tile, j * tile:(j + 1) * tile]
     pl.semaphore_wait(barrier, n_rows + 1)
-    own_squares[...] = jnp.zeros_like(own_squares)
-    for b in range(2):
-        wide = blocks[0, b].astype(F32)
-        sums = jnp.sum(wide * wide, axis=0, keepdims=True)
-        for i in range(2):
-            own_squares[2 * b + i:2 * b + i + 1, :] = sums[:, i * tile:(i + 1) * tile]
-
     def spread_squares(k):
         return remote(own_squares, squares.at[k - 1], sq_send.at[k], sq_recv.at[k], rows=peer(k))
 
     def send_squares():
+        own_squares[...] = jnp.zeros_like(own_squares)
+        for b in range(2):
+            wide = blocks[0, b].astype(F32)
+            sums = jnp.sum(wide * wide, axis=0, keepdims=True)
+            for i in range(2):
+                own_squares[2 * b + i:2 * b + i + 1, :] = sums[:, i * tile:(i + 1) * tile]
         for k in range(1, n_rows):
             start(functools.partial(spread_squares, k))
 
-    acc, rows_of = scatter_rows(0, part0, landed0, send_squares)
-    gather_rows_by_axes(0, acc, rows_of, gram0)
+    acc, rows_of = scatter_rows(0, part0, landed0)
+    gather_rows(0, acc, rows_of, gram0, send_squares)
     for n, (a, b, (i, j)) in enumerate(spots):
         row, col = a * half + i * tile, b * half + j * tile
         piece = gram0[n * tile:(n + 1) * tile, :].astype(F32)
@@ -309,14 +298,14 @@
     rotate_and_send(0, size)
 
     part[0] = cross_of(1).astype(BF16)
-    acc, rows_of = scatter_rows(1, part.at[0], landed.at[0], lambda: spread_diag(0))
-    gather_rows(0, acc, rows_of, cross.at[0])
+    acc, rows_of = scatter_rows(1, part.at[0], landed.at[0], lambda: send_diag(0))
+    gather_rows(1, acc, rows_of, cross.at[0], lambda: spread_diag(0))
     finish_gram(0, cross[0])
     rotate_and_send(1, solve(1))
 
     part[1] = cross_of(2).astype(BF16)
-    acc, rows_of = scatter_rows(2, part.at[1], landed.at[1], lambda: spread_diag(1))
-    gather_rows(1, acc, rows_of, cross.at[1])
+    acc, rows_of = scatter_rows(2, part.at[1], landed.at[1], lambda: send_diag(1))
+    gather_rows(2, acc, rows_of, cross.at[1], lambda: spread_diag(1))
     finish_gram(1, cross[1])
     solve(2)
     for c in range(CHUNKS):
@@ -371,7 +360,6 @@
             dma((3,)),
             *pairs(n_rows),
             *pairs(steps, n_rows),
-            *pairs(moves, n_rows),
             *pairs(steps, n_rows // Y_SIZE),
             *pairs(steps, n_rows // Y_SIZE, Y_SIZE),
             *pairs(moves, 2, CHUNKS),

time: 122 us -> 127 us (1.041)
  Pallas kernels: 120 us -> 125 us
    pallas_call x1, Pallas kernels: 120 us -> 125 us  [body(): pl.pallas_call(functools.partial(kernel, n_factor, n_rows, steps), out_sh...]
where the time goes in v4:
time: 127 us
  Pallas kernels  125 us (98%)
  local copies, waits for them, and re-layouts  1.66 us (1%)
    pallas_call x1, Pallas kernels, body(): pl.pallas_call(functools.partial(kernel, n_factor, n_rows, steps), out_sh...  125 us

profile of v4, /device:TPU:1, one launch (start us, length us, event | category | flops | bytes accessed | tf_op | source)
XLA Modules:
  0.0 126.8 jit_solution(5347353228339017992)
XLA Ops:
  0.0 0.0 copy-start
  0.0 0.7 copy-done
  0.7 125.1 %jacobi.1 = bf16[1024,512]{1,0:T(8,128)(2,1)S(1)} custom-call(bf16[1024,512]{1,0:T(8,128)(2,1)} %working.1, s32[3,1,512]{2,1,0:T(1,128)S(1)} %copy-done), custom_call_target="tpu_custom_call" | custom-call | flops 3221225472 | bytes 2097152 | tf_op jit(solution)/shard_map/jacobi/pallas_call | solution.py:333
  125.8 1.0 copy.4
Async XLA Ops:
  0.0 0.7 copy-start

commit v5 on v4

--- a/solution.py
+++ b/solution.py
@@ -38,7 +38,7 @@
 def kernel(n_factor, n_rows, steps, working, levels_in, out,
            levels, blocks, outs, part0, part, landed0, landed, gram0, cross,
            own_squares, squares, diag, diag_stage, line, line_stage, gram, narrow, narrow_rest, square, square_rest, rotation,
-           in_sem, sq_send, sq_recv, rs_send, rs_recv, agz_send, agz_recv, agy_send, agy_recv, mv_send, mv_recv,
+           in_sem, sq_send, sq_recv, rs_send, rs_recv, ag_send, ag_recv, agz_send, agz_recv, agy_send, agy_recv, mv_send, mv_recv,
            dg_send, dg_recv, df_send, df_recv, ln_send, ln_recv):
     f, r = lax.axis_index("factor"), lax.axis_index("rows")
     y = lax.rem(r, Y_SIZE)
@@ -108,6 +108,18 @@
         return acc, rows_of
 
     def gather_rows(s, acc, rows_of, total, meanwhile):
+        def gather(k, device):
+            return remote(total.at[rows_of(device)], total.at[rows_of(device)],
+                          ag_send.at[s, k], ag_recv.at[s, k], rows=peer(k))
+
+        total[rows_of(r), :] = acc.astype(total.dtype)
+        for k in range(1, n_rows):
+            start(functools.partial(gather, k, r))
+        meanwhile()
+        for k in range(1, n_rows):
+            gather(k, peer_back(k)).wait_recv()
+
+    def gather_rows_by_axes(s, acc, rows_of, total, meanwhile):
         def along_z(k, device):
             return remote(total.at[rows_of(device)], total.at[rows_of(device)], agz_send.at[s, k], agz_recv.at[s, k],
                           rows=lax.rem(z + k, z_size) * Y_SIZE + y)
@@ -280,7 +292,7 @@
             start(functools.partial(spread_squares, k))
 
     acc, rows_of = scatter_rows(0, part0, landed0)
-    gather_rows(0, acc, rows_of, gram0, send_squares)
+    gather_rows_by_axes(0, acc, rows_of, gram0, send_squares)
     for n, (a, b, (i, j)) in enumerate(spots):
         row, col = a * half + i * tile, b * half + j * tile
         piece = gram0[n * tile:(n + 1) * tile, :].astype(F32)
@@ -299,13 +311,13 @@
 
     part[0] = cross_of(1).astype(BF16)
     acc, rows_of = scatter_rows(1, part.at[0], landed.at[0], lambda: send_diag(0))
-    gather_rows(1, acc, rows_of, cross.at[0], lambda: spread_diag(0))
+    gather_rows(0, acc, rows_of, cross.at[0], lambda: spread_diag(0))
     finish_gram(0, cross[0])
     rotate_and_send(1, solve(1))
 
     part[1] = cross_of(2).astype(BF16)
     acc, rows_of = scatter_rows(2, part.at[1], landed.at[1], lambda: send_diag(1))
-    gather_rows(2, acc, rows_of, cross.at[1], lambda: spread_diag(1))
+    gather_rows(1, acc, rows_of, cross.at[1], lambda: spread_diag(1))
     finish_gram(1, cross[1])
     solve(2)
     for c in range(CHUNKS):
@@ -360,6 +372,7 @@
             dma((3,)),
             *pairs(n_rows),
             *pairs(steps, n_rows),
+            *pairs(moves, n_rows),
             *pairs(steps, n_rows // Y_SIZE),
             *pairs(steps, n_rows // Y_SIZE, Y_SIZE),
             *pairs(moves, 2, CHUNKS),

time: 127 us -> 122 us (0.961)
  Pallas kernels: 125 us -> 120 us
    pallas_call x1, Pallas kernels: 125 us -> 120 us  [body(): pl.pallas_call(functools.partial(kernel, n_factor, n_rows, steps), out_sh...]
where the time goes in v5:
time: 122 us; the launch traced here: 121 us
  Pallas kernels  120 us (98%)
  local copies, waits for them, and re-layouts  1.66 us (1%)
    pallas_call x1, Pallas kernels, body(): pl.pallas_call(functools.partial(kernel, n_factor, n_rows, steps), out_sh...  120 us

profile of v5, /device:TPU:1, one launch (start us, length us, event | category | flops | bytes accessed | tf_op | source)
XLA Modules:
  0.0 121.4 jit_solution(4816265700812930035)
XLA Ops:
  0.0 0.0 copy-start
  0.0 0.7 copy-done
  0.7 119.7 %jacobi.1 = bf16[1024,512]{1,0:T(8,128)(2,1)S(1)} custom-call(bf16[1024,512]{1,0:T(8,128)(2,1)} %working.1, s32[3,1,512]{2,1,0:T(1,128)S(1)} %copy-done), custom_call_target="tpu_custom_call" | custom-call | flops 3221225472 | bytes 2097152 | tf_op jit(solution)/shard_map/jacobi/pallas_call | solution.py:345
  120.4 1.0 copy.4
Async XLA Ops:
  0.0 0.7 copy-start

commit v6 on v5

--- a/solution.py
+++ b/solution.py
@@ -11,7 +11,7 @@
 MESH = pl.DeviceIdType.MESH
 F32, BF16 = jnp.float32, jnp.bfloat16
 Y_SIZE = 4
-CHUNKS = 4
+CHUNKS = 8
 
 
 def inner_rows(left, right):

time: 122 us -> 122 us (level)
  no operation moved by 1% of the time
where the time goes in v6:
time: 122 us; the launch traced here: 121 us
  Pallas kernels  120 us (98%)
  local copies, waits for them, and re-layouts  1.66 us (1%)
    pallas_call x1, Pallas kernels, body(): pl.pallas_call(functools.partial(kernel, n_factor, n_rows, steps), out_sh...  120 us

profile of v6, /device:TPU:1, one launch (start us, length us, event | category | flops | bytes accessed | tf_op | source)
XLA Modules:
  0.0 121.4 jit_solution(2050873165042627609)
XLA Ops:
  0.0 0.0 copy-start
  0.0 0.7 copy-done
  0.7 119.7 %jacobi.1 = bf16[1024,512]{1,0:T(8,128)(2,1)S(1)} custom-call(bf16[1024,512]{1,0:T(8,128)(2,1)} %working.1, s32[3,1,512]{2,1,0:T(1,128)S(1)} %copy-done), custom_call_target="tpu_custom_call" | custom-call | flops 3221225472 | bytes 2097152 | tf_op jit(solution)/shard_map/jacobi/pallas_call | solution.py:345
  120.4 1.0 copy.4
Async XLA Ops:
  0.0 0.7 copy-start
